TPU v7x, 32 devices: a whole 2x2x4 slice. The times are simulated.
32 devices in a mesh: tm: 8 (over y, x, core), col: 4 (over z).
Axes of the slice: x: 2, y: 2, z: 4, core: 2. Of those that a mesh axis runs over, the one named last changes fastest.
Arguments:
- readings: bfloat16 [64, 64, 512], P('tm', 'col'), may hold values from -6 to 6
- block_owner: int32 [64, 1], P('tm'), may hold values from 0 to 7; in each aligned block of 8 rows (0 to 7, 8 to 15, ...) at most 4 rows name the same one
- block_offset: int32 [64], P('tm'), may hold values from 0 to 7
- initial_mean: float32 [64, 512], P('col'), may hold values from -6 to 6
- transition: float32 [512, 512], replicated, may hold values from -1 to 1
- shrink_rate: float32 [512], replicated, may hold values from 0.003125 to 0.078125
- input_map: float32 [512, 512], replicated, may hold values from -0.0625 to 0.0625
- smoother_gain: float32 [512, 512], replicated, may hold values from -1 to 1
Outputs:
- filtered: float32 [64, 64, 512], P('tm', 'col')
- smoothed: float32 [64, 64, 512], P('tm', 'col')
Inputs may be any that keep to these rules, and one draw needn't show every extreme that they name: `block_owner`: the blocks of one index of tm name one owner at most 4 times, and in every draw some owner exactly 4 times.
All inputs are finite; a program needn't handle non-finite values.
Results may differ from a plain program's by a relative error of at most 0.0003.
Values may be sent and summed in bfloat16 or wider, within the bound.
A program may use at most 128 MiB of HBM per device.

v0:
```python
import functools
import jax
import jax.numpy as jnp
from jax import lax
from jax.experimental import pallas as pl
from jax.experimental.pallas import tpu as pltpu
from jax.sharding import PartitionSpec as P

STEPS_DEV = 8
BF = jnp.bfloat16
F32 = jnp.float32


def halves(x):
    hi = x.astype(BF)
    return hi, (x - hi.astype(F32)).astype(BF)


def dot(a, b):
    return jnp.dot(a, b, preferred_element_type=F32)


def product(x, hi_ref, lo_ref):
    rows = x.shape[0]
    hi, lo = halves(x)
    both = dot(jnp.concatenate([hi, lo], axis=0), hi_ref[...])
    return both[:rows] + both[rows:] + dot(hi, lo_ref[...])


def split_into(x, hi_ref, lo_ref):
    hi, lo = halves(x)
    hi_ref[...] = hi
    lo_ref[...] = lo


def square_into(x_ref, y_hi, y_lo, out):
    width = x_ref.shape[0]
    chunk = 128

    @pl.loop(0, width // chunk)
    def _(i):
        rows = pl.ds(pl.multiple_of(i * chunk, chunk), chunk)
        out(rows, product(x_ref[rows, :], y_hi, y_lo))


def kernel(
    slabs, levels, readings, target, initial, transition, shrink, input_map, gain,
    filtered, smoothed,
    a_hi, a_lo, w_hi, w_lo, b_hi, b_lo, g_hi, g_lo, square,
    drive, factor, means, mixed, pairs, quads, sums,
):
    me = lax.axis_index("tm")
    width = transition.shape[0]
    batch = initial.shape[0]
    steps = slabs * STEPS_DEV
    per = STEPS_DEV * batch
    split_into(transition[...], a_hi, a_lo)
    split_into(input_map[...], w_hi, w_lo)
    split_into(gain[...], g_hi.at[0], g_lo.at[0])

    def put_blend(rows, value):
        row = lax.broadcasted_iota(jnp.int32, value.shape, 0) + rows.start
        col = lax.broadcasted_iota(jnp.int32, value.shape, 1)
        blend = jnp.where(row == col, 1.0, 0.0) - value
        split_into(blend, b_hi.at[rows, :], b_lo.at[rows, :])

    square_into(transition, g_hi.at[0], g_lo.at[0], put_blend)

    for level in range(1, levels):
        def put_power(rows, value):
            square[level % 2, rows, :] = value
            split_into(value, g_hi.at[level, rows, :], g_lo.at[level, rows, :])

        source = gain if level == 1 else square.at[(level - 1) % 2]
        square_into(source, g_hi.at[level - 1], g_lo.at[level - 1], put_power)

    count = jnp.zeros((steps, 1), F32)
    for slab in range(slabs):
        hit = lax.broadcasted_iota(jnp.int32, (steps, per), 0) * batch == target[pl.ds(slab, 1), :]
        count += jnp.sum(jnp.where(hit, 1.0, 0.0), axis=1, keepdims=True)
    factor[...] = jnp.exp(-count * shrink[...])

    @pl.loop(0, slabs)
    def _(to):
        inflow = jnp.zeros((per, width), F32)
        row = lax.broadcasted_iota(jnp.int32, (per, per), 0) + to * per
        for slab in range(slabs):
            pick = jnp.where(row == target[pl.ds(slab, 1), :], 1.0, 0.0).astype(BF)
            inflow += dot(pick, readings[pl.ds(slab * per, per), :])
        pushes = product(inflow, w_hi, w_lo)
        drive[pl.ds(to * STEPS_DEV, STEPS_DEV)] = pushes.reshape(STEPS_DEV, batch, width)

    def forward(step, mean):
        mean = product(mean, a_hi, a_lo) * factor[pl.ds(step, 1), :] + drive[step]
        means[step] = mean
        return mean

    lax.fori_loop(0, steps, forward, initial[...], unroll=4)
    filtered[...] = means[pl.ds(me * STEPS_DEV, STEPS_DEV)]

    @pl.loop(0, slabs)
    def _(slab):
        part = pl.ds(slab * STEPS_DEV, STEPS_DEV)
        mix = product(means[part].reshape(per, width), b_hi, b_lo)
        mixed[part] = mix.reshape(STEPS_DEV, batch, width)

    mixed[steps - 1] = means[steps - 1]

    def fold(values, level):
        number = values.shape[0] // 2
        values = values.reshape(number, 2, batch, width)
        odd = values[:, 1].reshape(number * batch, width)
        moved = product(odd, g_hi.at[level], g_lo.at[level])
        return values[:, 0] + moved.reshape(number, batch, width)

    @pl.loop(0, slabs // 2)
    def _(i):
        part = pl.ds(i * 2 * STEPS_DEV, 2 * STEPS_DEV)
        pairs[pl.ds(i * STEPS_DEV, STEPS_DEV)] = fold(mixed[part], 0)

    quads[...] = fold(pairs[...], 1)
    sums[pl.ds(0, slabs)] = fold(quads[...], 2)
    sums[pl.ds(slabs, slabs)] = jnp.zeros((slabs, batch, width), F32)
    later = sums[pl.ds(me + 1, slabs)]
    for level in range(3, levels):
        later = fold(later, level)
    carry = later[0]

    def back(state, level):
        return product(state, g_hi.at[level], g_lo.at[level])

    at0 = sums[me] + back(carry, 3)
    at4 = quads[me * 2 + 1] + back(carry, 2)
    two = back(jnp.concatenate([at4, carry], axis=0), 1)
    at2 = pairs[me * 4 + 1] + two[:batch]
    at6 = pairs[me * 4 + 3] + two[batch:]
    one = back(jnp.concatenate([at2, at4, at6, carry], axis=0), 0)
    base = me * STEPS_DEV
    smoothed[0] = at0
    smoothed[2] = at2
    smoothed[4] = at4
    smoothed[6] = at6
    for i in range(4):
        smoothed[2 * i + 1] = mixed[base + 2 * i + 1] + one[i * batch:(i + 1) * batch]


def per_device(
    readings, block_owner, block_offset, initial_mean, transition, shrink_rate, input_map, smoother_gain
):
    slabs = lax.axis_size("tm")
    blocks, batch, width = readings.shape
    steps = slabs * STEPS_DEV
    levels = 3 + (slabs - 1).bit_length()
    step = block_owner[:, 0] * STEPS_DEV + block_offset
    target = (step[:, None] * batch + jnp.arange(batch, dtype=jnp.int32)[None, :]).reshape(1, -1)
    readings = lax.all_gather(readings.reshape(-1, width), "tm", axis=0, tiled=True)
    target = lax.all_gather(target, "tm", axis=0, tiled=True)
    out = jax.ShapeDtypeStruct((STEPS_DEV, batch, width), F32)
    return pl.pallas_call(
        functools.partial(kernel, slabs, levels),
        out_shape=(out, out),
        in_specs=[pl.BlockSpec(memory_space=pltpu.VMEM)] * 7,
        out_specs=[pl.BlockSpec(memory_space=pltpu.VMEM)] * 2,
        scratch_shapes=[pltpu.VMEM((width, width), BF)] * 6
        + [pltpu.VMEM((levels, width, width), BF)] * 2
        + [
            pltpu.VMEM((2, width, width), F32),
            pltpu.VMEM((steps, batch, width), F32),
            pltpu.VMEM((steps, width), F32),
            pltpu.VMEM((steps, batch, width), F32),
            pltpu.VMEM((steps, batch, width), F32),
            pltpu.VMEM((steps // 2, batch, width), F32),
            pltpu.VMEM((steps // 4, batch, width), F32),
            pltpu.VMEM((2 * slabs, batch, width), F32),
        ],
        compiler_params=pltpu.CompilerParams(vmem_limit_bytes=56 * 2**20),
    )(readings, target, initial_mean, transition, shrink_rate.reshape(1, -1), input_map, smoother_gain)


def solution(mesh):
    in_specs = (P("tm", "col", None), P("tm", None), P("tm"), P("col", None), P(), P(), P(), P())
    out_specs = (P("tm", "col", None), P("tm", "col", None))
    return jax.shard_map(
        per_device, mesh=mesh, in_specs=in_specs, out_specs=out_specs, check_vma=False
    )
```

profile of v0, /device:TPU:1, one launch (start us, length us, event | category | flops | bytes accessed | tf_op | source)
XLA Modules:
  0.0 83.8 jit_solution(13770658475706509950)
XLA Ops:
  7.2 0.0 all-gather.3.cloned.1.call-start
  7.2 0.0 copy-start
  7.2 0.0 copy-start.1
  7.2 0.7 all-gather.3.cloned.1.call-update
  7.9 0.0 copy-done
  7.9 0.0 copy-done.1
  7.9 0.1 iota_add_fusion
  8.0 0.1 reshape.39
  8.1 10.7 %all-gather = s32[8,1,128]{2,1,0:T(1,128)} all-gather(s32[1,1,128]{2,1,0:T(1,128)S(1)} %reshape.39), channel_id=1, replica_groups=mesh['tm'=8,'col'=4] {'tm'}, dimensions={0}, use_global_device_ids=true | all-gather | bytes 4608 | tf_op jit(solution)/shard_map/all_gather | solution.py:157
  18.8 17.1 %all-gather.3.cloned.1.call-done.readings = bf16[1024,512]{1,0:T(8,128)(2,1)} async-done(((bf16[128,512]{1,0:T(8,128)(2,1)}), bf16[1024,512]{1,0:T(8,128)(2,1)}) %all-gather.3.cloned.1.call-update) | async-done | bytes 1048592 | tf_op jit(solution)/shard_map/all_gather | solution.py:156
  35.9 41.0 %shard_map.95 = (f32[8,16,512]{2,1,0:T(8,128)}, f32[8,16,512]{2,1,0:T(8,128)}) custom-call(bf16[1024,512]{1,0:T(8,128)(2,1)} %all-gather.3.cloned.1.call-done.readings, s32[8,128]{1,0:T(8,128)} %bitcast.8, f32[16,512]{1,0:T(8,128)} %initial.1, f32[512,512]{1,0:T(8,128)} %transition.1, f32[1,512]{1,0:T(1,128)} %bitcast.9, f32[512,512]{1,0:T(8,128)} %input_map.1, ...), custom_call_target="tpu_custom_call" | custom-call | tf_op jit(solution)/shard_map/pallas_call | solution.py:159
  (1 shorter events, 0.0 us)
Async XLA Ops:
  7.2 28.8 %all-gather.3.cloned.1.call-start = ((), (), s32[]{:S(2)}) async-start(), calls=%async_computation | async-start | bytes 1179648 | tf_op jit(solution)/shard_map/all_gather | solution.py:156
  7.2 0.7 copy-start
  7.2 0.7 copy-start.1
Sparse Core Ops, SparseCore 0:
  9.9 25.9 all-gather.2
where the time goes:
time: 84.1 us; the launch traced here: 83.8 us
  Pallas kernels  41 us (49%)
  waiting for transfers between devices  17.8 us (21%)
  between operations  14.1 us (17%)
  blocking collectives  10.7 us (13%)
    pallas_call x1, Pallas kernels, per_device(): pl.pallas_call(functools.partial(kernel, slabs, levels), out_shape=(out,...  41 us
    all_gather x1, waiting for transfers between devices, per_device(): lax.all_gather(readings.reshape(-1, width), 'tm', axis=0, tiled=True)  17.1 us
    all_gather x1, blocking collectives, per_device(): target = lax.all_gather(target, 'tm', axis=0, tiled=True)  10.7 us
  transfers between devices with their start and end apart: 1, of which 1 were waited for; matrix products, arithmetic and copies ran while one was open for 0% of the time, Pallas kernels for 0%

commit v1 on v0

--- a/solution.py
+++ b/solution.py
@@ -9,6 +9,7 @@
 STEPS_DEV = 8
 BF = jnp.bfloat16
 F32 = jnp.float32
+MESH = pl.DeviceIdType.MESH
 
 
 def halves(x):
@@ -44,19 +45,75 @@
 
 
 def kernel(
-    slabs, levels, readings, target, initial, transition, shrink, input_map, gain,
+    slabs, levels, readings, owner, offset, initial, shrink, transition_in, input_map_in, gain_in,
     filtered, smoothed,
+    arrived, target, transition, input_map, gain,
     a_hi, a_lo, w_hi, w_lo, b_hi, b_lo, g_hi, g_lo, square,
     drive, factor, means, mixed, pairs, quads, sums,
+    load_sem, own_sem, send_sem, recv_sem, send_target_sem, recv_target_sem,
 ):
     me = lax.axis_index("tm")
     width = transition.shape[0]
     batch = initial.shape[0]
     steps = slabs * STEPS_DEV
     per = STEPS_DEV * batch
+
+    barrier = pltpu.get_barrier_semaphore()
+    for hop in range(1, slabs):
+        pl.semaphore_signal(
+            barrier, inc=1, device_id={"tm": lax.rem(me + hop, slabs)}, device_id_type=MESH
+        )
+    loads = [
+        pltpu.make_async_copy(source, into, load_sem.at[i])
+        for i, (source, into) in enumerate(
+            ((gain_in, gain), (transition_in, transition), (input_map_in, input_map))
+        )
+    ]
+    for load in loads:
+        load.start()
+    mine = pl.ds(me * STEPS_DEV, STEPS_DEV)
+    own = pltpu.make_async_copy(readings, arrived.at[mine], own_sem)
+    own.start()
+
+    blocks = owner.shape[1]
+    square_shape = (blocks, blocks)
+    diagonal = lax.broadcasted_iota(jnp.int32, square_shape, 0) == lax.broadcasted_iota(
+        jnp.int32, square_shape, 1
+    )
+    step = (owner[...] * STEPS_DEV + offset[...]).astype(F32)
+    step = jnp.sum(jnp.where(diagonal, step, 0.0), axis=1, keepdims=True)
+    lane = lax.broadcasted_iota(jnp.int32, (blocks, per), 1)
+    block = lax.broadcasted_iota(jnp.int32, (blocks, per), 0)
+    inside = lane - block * batch
+    here = jnp.logical_and(inside >= 0, inside < batch)
+    row = step * batch + inside.astype(F32)
+    target[me] = jnp.sum(jnp.where(here, row, 0.0), axis=0, keepdims=True)
+
+    pl.semaphore_wait(barrier, slabs - 1)
+    copies = []
+    for hop in range(1, slabs):
+        peer = {"tm": lax.rem(me + hop, slabs)}
+        copies.append(
+            pltpu.make_async_remote_copy(
+                readings, arrived.at[mine], send_sem.at[hop], recv_sem.at[hop],
+                device_id=peer, device_id_type=MESH,
+            )
+        )
+        copies.append(
+            pltpu.make_async_remote_copy(
+                target.at[me], target.at[me], send_target_sem.at[hop], recv_target_sem.at[hop],
+                device_id=peer, device_id_type=MESH,
+            )
+        )
+    for copy in copies:
+        copy.start()
+
+    loads[0].wait()
+    split_into(gain[...], g_hi.at[0], g_lo.at[0])
+    loads[1].wait()
     split_into(transition[...], a_hi, a_lo)
+    loads[2].wait()
     split_into(input_map[...], w_hi, w_lo)
-    split_into(gain[...], g_hi.at[0], g_lo.at[0])
 
     def put_blend(rows, value):
         row = lax.broadcasted_iota(jnp.int32, value.shape, 0) + rows.start
@@ -74,19 +131,26 @@
         source = gain if level == 1 else square.at[(level - 1) % 2]
         square_into(source, g_hi.at[level - 1], g_lo.at[level - 1], put_power)
 
+    own.wait()
+    for copy in copies:
+        copy.wait_recv()
+
     count = jnp.zeros((steps, 1), F32)
     for slab in range(slabs):
-        hit = lax.broadcasted_iota(jnp.int32, (steps, per), 0) * batch == target[pl.ds(slab, 1), :]
+        hit = lax.broadcasted_iota(jnp.int32, (steps, per), 0)
+        behind = target[slab] - hit.astype(F32) * batch
+        hit = jnp.logical_and(behind >= 0.0, behind < batch)
         count += jnp.sum(jnp.where(hit, 1.0, 0.0), axis=1, keepdims=True)
+    count = count / batch
     factor[...] = jnp.exp(-count * shrink[...])
 
     @pl.loop(0, slabs)
     def _(to):
         inflow = jnp.zeros((per, width), F32)
-        row = lax.broadcasted_iota(jnp.int32, (per, per), 0) + to * per
+        row = (lax.broadcasted_iota(jnp.int32, (per, per), 0) + to * per).astype(F32)
         for slab in range(slabs):
-            pick = jnp.where(row == target[pl.ds(slab, 1), :], 1.0, 0.0).astype(BF)
-            inflow += dot(pick, readings[pl.ds(slab * per, per), :])
+            pick = jnp.where(row == target[slab], 1.0, 0.0).astype(BF)
+            inflow += dot(pick, arrived[pl.ds(slab * STEPS_DEV, STEPS_DEV)].reshape(per, width))
         pushes = product(inflow, w_hi, w_lo)
         drive[pl.ds(to * STEPS_DEV, STEPS_DEV)] = pushes.reshape(STEPS_DEV, batch, width)
 
@@ -143,6 +207,9 @@
     for i in range(4):
         smoothed[2 * i + 1] = mixed[base + 2 * i + 1] + one[i * batch:(i + 1) * batch]
 
+    for copy in copies:
+        copy.wait_send()
+
 
 def per_device(
     readings, block_owner, block_offset, initial_mean, transition, shrink_rate, input_map, smoother_gain
@@ -150,18 +217,22 @@
     slabs = lax.axis_size("tm")
     blocks, batch, width = readings.shape
     steps = slabs * STEPS_DEV
+    per = STEPS_DEV * batch
     levels = 3 + (slabs - 1).bit_length()
-    step = block_owner[:, 0] * STEPS_DEV + block_offset
-    target = (step[:, None] * batch + jnp.arange(batch, dtype=jnp.int32)[None, :]).reshape(1, -1)
-    readings = lax.all_gather(readings.reshape(-1, width), "tm", axis=0, tiled=True)
-    target = lax.all_gather(target, "tm", axis=0, tiled=True)
     out = jax.ShapeDtypeStruct((STEPS_DEV, batch, width), F32)
     return pl.pallas_call(
         functools.partial(kernel, slabs, levels),
         out_shape=(out, out),
-        in_specs=[pl.BlockSpec(memory_space=pltpu.VMEM)] * 7,
+        in_specs=[pl.BlockSpec(memory_space=pl.ANY)]
+        + [pl.BlockSpec(memory_space=pltpu.VMEM)] * 4
+        + [pl.BlockSpec(memory_space=pl.ANY)] * 3,
         out_specs=[pl.BlockSpec(memory_space=pltpu.VMEM)] * 2,
-        scratch_shapes=[pltpu.VMEM((width, width), BF)] * 6
+        scratch_shapes=[
+            pltpu.VMEM((slabs * blocks, batch, width), BF),
+            pltpu.VMEM((slabs, 1, per), F32),
+        ]
+        + [pltpu.VMEM((width, width), F32)] * 3
+        + [pltpu.VMEM((width, width), BF)] * 6
         + [pltpu.VMEM((levels, width, width), BF)] * 2
         + [
             pltpu.VMEM((2, width, width), F32),
@@ -172,9 +243,17 @@
             pltpu.VMEM((steps // 2, batch, width), F32),
             pltpu.VMEM((steps // 4, batch, width), F32),
             pltpu.VMEM((2 * slabs, batch, width), F32),
-        ],
-        compiler_params=pltpu.CompilerParams(vmem_limit_bytes=56 * 2**20),
-    )(readings, target, initial_mean, transition, shrink_rate.reshape(1, -1), input_map, smoother_gain)
+            pltpu.SemaphoreType.DMA((3,)),
+            pltpu.SemaphoreType.DMA,
+        ]
+        + [pltpu.SemaphoreType.DMA((slabs,))] * 4,
+        compiler_params=pltpu.CompilerParams(
+            vmem_limit_bytes=56 * 2**20, collective_id=0, has_side_effects=True
+        ),
+    )(
+        readings, block_owner.reshape(1, -1), block_offset.reshape(1, -1), initial_mean,
+        shrink_rate.reshape(1, -1), transition, input_map, smoother_gain,
+    )
 
 
 def solution(mesh):

time: 84.1 us -> 50.3 us (0.60)
  waiting for transfers between devices: 17.8 us -> 0 us
  between operations: 14.1 us -> 0.65 us
  blocking collectives: 10.7 us -> 0 us
  Pallas kernels: 41 us -> 47 us
  local copies, waits for them, and re-layouts: 0.09 us -> 2.42 us
    all_gather x1 -> x0, waiting for transfers between devices: 17.1 us -> none  [per_device(): lax.all_gather(readings.reshape(-1, width), 'tm', axis=0, tiled=True)]
    all_gather x1 -> x0, blocking collectives: 10.7 us -> none  [per_device(): target = lax.all_gather(target, 'tm', axis=0, tiled=True)]
    pallas_call x1, Pallas kernels: 41 us -> 47 us  [per_device(): pl.pallas_call(functools.partial(kernel, slabs, levels), out_shape=(out,...]
    unnamed x5 -> x4, local copies, waits for them, and re-layouts: 0.09 us -> 2.42 us
  transfers between devices with their start and end apart: 1 -> 0, of which waited for: 1 -> 0; matrix products, arithmetic and copies ran while one was open for 0% -> 0% of each run, Pallas kernels for 0% -> 0%
where the time goes in v1:
time: 50.3 us; the launch traced here: 50.1 us
  Pallas kernels  47 us (93%)
  local copies, waits for them, and re-layouts  2.42 us (5%)
  between operations  0.65 us (1%)
    pallas_call x1, Pallas kernels, per_device(): pl.pallas_call(functools.partial(kernel, slabs, levels), out_shape=(out,...  47 us
    unnamed x4, local copies, waits for them, and re-layouts  2.42 us

profile of v1, /device:TPU:1, one launch (start us, length us, event | category | flops | bytes accessed | tf_op | source)
XLA Modules:
  0.0 50.1 jit_solution(4847912659482305158)
XLA Ops:
  0.6 47.0 %shard_map.95 = (f32[8,16,512]{2,1,0:T(8,128)}, f32[8,16,512]{2,1,0:T(8,128)}) custom-call(bf16[8,16,512]{2,1,0:T(8,128)(2,1)} %readings.1, s32[1,8]{1,0:T(1,128)} %bitcast.4, s32[1,8]{1,0:T(1,128)} %bitcast.5, f32[16,512]{1,0:T(8,128)} %initial.1, f32[1,512]{1,0:T(1,128)} %bitcast.3, f32[512,512]{1,0:T(8,128)} %transition_in.1, f32[512,512]{1,0:T(8,128)} %input_map_in.1, ...), custom_call_target="tpu_custom_call" | custom-call | tf_op jit(solution)/shard_map/pallas_call | solution.py:223
  47.6 0.0 copy-start
  47.7 1.7 %copy.12 = f32[8,16,512]{2,1,0:T(8,128)} copy(f32[8,16,512]{2,1,0:T(8,128)} %get-tuple-element.4) | data formatting | bytes 524288
  49.4 0.0 copy-done
  49.4 0.7 %copy.13 = f32[8,16,512]{2,1,0:T(8,128)} copy(f32[8,16,512]{2,1,0:T(8,128)S(1)} %copy-done) | data formatting | bytes 524288
Async XLA Ops:
  47.6 1.7 %copy-start = (f32[8,16,512]{2,1,0:T(8,128)S(1)}, f32[8,16,512]{2,1,0:T(8,128)}, u32[]{:S(2)}) copy-start(f32[8,16,512]{2,1,0:T(8,128)} %get-tuple-element.5) | copy-start | bytes 786436

commit v2 on v1

--- a/solution.py
+++ b/solution.py
@@ -49,7 +49,7 @@
     filtered, smoothed,
     arrived, target, transition, input_map, gain,
     a_hi, a_lo, w_hi, w_lo, b_hi, b_lo, g_hi, g_lo, square,
-    drive, factor, means, mixed, pairs, quads, sums,
+    inflow, drive, factor, means, mixed, pairs, quads, sums,
     load_sem, own_sem, send_sem, recv_sem, send_target_sem, recv_target_sem,
 ):
     me = lax.axis_index("tm")
@@ -90,23 +90,44 @@
     target[me] = jnp.sum(jnp.where(here, row, 0.0), axis=0, keepdims=True)
 
     pl.semaphore_wait(barrier, slabs - 1)
-    copies = []
-    for hop in range(1, slabs):
-        peer = {"tm": lax.rem(me + hop, slabs)}
-        copies.append(
+    duos = slabs // 2
+    duo, side = lax.div(me, 2), lax.rem(me, 2)
+    sibling = {"tm": duo * 2 + 1 - side}
+
+    def block_of(hop):
+        source = lax.rem(duo + duos - hop, duos) * 2 + side
+        return arrived.at[pl.ds(source * STEPS_DEV, STEPS_DEV)]
+
+    directs, forwards, labels = [], [None], []
+    for hop in range(duos):
+        peer = sibling if hop == 0 else {"tm": lax.rem(duo + hop, duos) * 2 + side}
+        directs.append(
             pltpu.make_async_remote_copy(
                 readings, arrived.at[mine], send_sem.at[hop], recv_sem.at[hop],
                 device_id=peer, device_id_type=MESH,
             )
         )
-        copies.append(
+    for hop in range(1, duos):
+        forwards.append(
+            pltpu.make_async_remote_copy(
+                block_of(hop), block_of(hop), send_sem.at[duos + hop], recv_sem.at[duos + hop],
+                device_id=sibling, device_id_type=MESH,
+            )
+        )
+    for hop in range(1, slabs):
+        labels.append(
             pltpu.make_async_remote_copy(
                 target.at[me], target.at[me], send_target_sem.at[hop], recv_target_sem.at[hop],
-                device_id=peer, device_id_type=MESH,
+                device_id={"tm": lax.rem(me + hop, slabs)}, device_id_type=MESH,
             )
         )
-    for copy in copies:
+    for copy in directs[1:] + directs[:1] + labels:
         copy.start()
+
+    def forward_block(hop):
+        if hop < duos:
+            directs[hop].wait_recv()
+            forwards[hop].start()
 
     loads[0].wait()
     split_into(gain[...], g_hi.at[0], g_lo.at[0])
@@ -121,19 +142,47 @@
         blend = jnp.where(row == col, 1.0, 0.0) - value
         split_into(blend, b_hi.at[rows, :], b_lo.at[rows, :])
 
+    def put_power(level, rows, value):
+        square[level % 2, rows, :] = value
+        split_into(value, g_hi.at[level, rows, :], g_lo.at[level, rows, :])
+
+    def power(level):
+        source = gain if level == 1 else square.at[(level - 1) % 2]
+        square_into(
+            source, g_hi.at[level - 1], g_lo.at[level - 1], functools.partial(put_power, level)
+        )
+
+    span = min(2 * per, steps * batch)
+
+    def add_duo(hop):
+        which = lax.rem(duo + duos - hop, duos) * 2
+        rows_of = jnp.concatenate([target[which], target[which + 1]], axis=1)
+
+        @pl.loop(0, steps * batch // span)
+        def _(i):
+            row = (lax.broadcasted_iota(jnp.int32, (span, 2 * per), 0) + i * span).astype(F32)
+            pick = jnp.where(row == rows_of, 1.0, 0.0).astype(BF)
+            values = arrived[pl.ds(which * STEPS_DEV, 2 * STEPS_DEV)].reshape(2 * per, width)
+            part = pl.ds(pl.multiple_of(i * span, span), span)
+            added = dot(pick, values)
+            inflow[part, :] = added if hop == 0 else inflow[part, :] + added
+
     square_into(transition, g_hi.at[0], g_lo.at[0], put_blend)
-
-    for level in range(1, levels):
-        def put_power(rows, value):
-            square[level % 2, rows, :] = value
-            split_into(value, g_hi.at[level, rows, :], g_lo.at[level, rows, :])
-
-        source = gain if level == 1 else square.at[(level - 1) % 2]
-        square_into(source, g_hi.at[level - 1], g_lo.at[level - 1], put_power)
-
+    forward_block(1)
+    power(1)
+    forward_block(2)
     own.wait()
-    for copy in copies:
-        copy.wait_recv()
+    directs[0].wait_recv()
+    for label in labels:
+        label.wait_recv()
+    add_duo(0)
+    for hop in range(3, duos):
+        forward_block(hop)
+    for level in range(2, levels):
+        power(level)
+    for hop in range(1, duos):
+        forwards[hop].wait_recv()
+        add_duo(hop)
 
     count = jnp.zeros((steps, 1), F32)
     for slab in range(slabs):
@@ -144,30 +193,37 @@
     count = count / batch
     factor[...] = jnp.exp(-count * shrink[...])
 
-    @pl.loop(0, slabs)
-    def _(to):
-        inflow = jnp.zeros((per, width), F32)
-        row = (lax.broadcasted_iota(jnp.int32, (per, per), 0) + to * per).astype(F32)
-        for slab in range(slabs):
-            pick = jnp.where(row == target[slab], 1.0, 0.0).astype(BF)
-            inflow += dot(pick, arrived[pl.ds(slab * STEPS_DEV, STEPS_DEV)].reshape(per, width))
-        pushes = product(inflow, w_hi, w_lo)
-        drive[pl.ds(to * STEPS_DEV, STEPS_DEV)] = pushes.reshape(STEPS_DEV, batch, width)
-
-    def forward(step, mean):
-        mean = product(mean, a_hi, a_lo) * factor[pl.ds(step, 1), :] + drive[step]
-        means[step] = mean
+    def push(slab):
+        rows = pl.ds(pl.multiple_of(slab * per, per), per)
+        value = product(inflow[rows, :], w_hi, w_lo)
+        drive[pl.ds(slab * STEPS_DEV, STEPS_DEV)] = value.reshape(STEPS_DEV, batch, width)
+
+    def mix(slab):
+        part = pl.ds(slab * STEPS_DEV, STEPS_DEV)
+        value = product(means[part].reshape(per, width), b_hi, b_lo)
+        mixed[part] = value.reshape(STEPS_DEV, batch, width)
+
+    def advance(slab, mean):
+        for i in range(STEPS_DEV):
+            step = slab * STEPS_DEV + i
+            mean = product(mean, a_hi, a_lo) * factor[pl.ds(step, 1), :] + drive[step]
+            means[step] = mean
         return mean
 
-    lax.fori_loop(0, steps, forward, initial[...], unroll=4)
-    filtered[...] = means[pl.ds(me * STEPS_DEV, STEPS_DEV)]
-
-    @pl.loop(0, slabs)
-    def _(slab):
-        part = pl.ds(slab * STEPS_DEV, STEPS_DEV)
-        mix = product(means[part].reshape(per, width), b_hi, b_lo)
-        mixed[part] = mix.reshape(STEPS_DEV, batch, width)
-
+    push(0)
+    push(1)
+    mean = advance(0, initial[...])
+
+    def body(slab, mean):
+        push(slab + 1)
+        mix(slab - 1)
+        return advance(slab, mean)
+
+    mean = lax.fori_loop(1, slabs - 1, body, mean)
+    mix(slabs - 2)
+    advance(slabs - 1, mean)
+    mix(slabs - 1)
+    filtered[...] = means[mine]
     mixed[steps - 1] = means[steps - 1]
 
     def fold(values, level):
@@ -207,7 +263,7 @@
     for i in range(4):
         smoothed[2 * i + 1] = mixed[base + 2 * i + 1] + one[i * batch:(i + 1) * batch]
 
-    for copy in copies:
+    for copy in directs + forwards[1:] + labels:
         copy.wait_send()
 
 
@@ -236,6 +292,7 @@
         + [pltpu.VMEM((levels, width, width), BF)] * 2
         + [
             pltpu.VMEM((2, width, width), F32),
+            pltpu.VMEM((steps * batch, width), F32),
             pltpu.VMEM((steps, batch, width), F32),
             pltpu.VMEM((steps, width), F32),
             pltpu.VMEM((steps, batch, width), F32),

time: 50.3 us -> 49.4 us (0.982)
  Pallas kernels: 47 us -> 45.7 us
    pallas_call x1, Pallas kernels: 47 us -> 45.7 us  [per_device(): pl.pallas_call(functools.partial(kernel, slabs, levels), out_shape=(out,...]
where the time goes in v2:
time: 49.4 us; the launch traced here: 48.8 us
  Pallas kernels  45.7 us (93%)
  local copies, waits for them, and re-layouts  2.42 us (5%)
  between operations  0.65 us (1%)
    pallas_call x1, Pallas kernels, per_device(): pl.pallas_call(functools.partial(kernel, slabs, levels), out_shape=(out,...  45.7 us
    unnamed x4, local copies, waits for them, and re-layouts  2.42 us

profile of v2, /device:TPU:1, one launch (start us, length us, event | category | flops | bytes accessed | tf_op | source)
XLA Modules:
  0.0 48.8 jit_solution(14080191464691693551)
XLA Ops:
  0.6 45.7 %shard_map.95 = (f32[8,16,512]{2,1,0:T(8,128)}, f32[8,16,512]{2,1,0:T(8,128)}) custom-call(bf16[8,16,512]{2,1,0:T(8,128)(2,1)} %readings.1, s32[1,8]{1,0:T(1,128)} %bitcast.4, s32[1,8]{1,0:T(1,128)} %bitcast.5, f32[16,512]{1,0:T(8,128)} %initial.1, f32[1,512]{1,0:T(1,128)} %bitcast.3, f32[512,512]{1,0:T(8,128)} %transition_in.1, f32[512,512]{1,0:T(8,128)} %input_map_in.1, ...), custom_call_target="tpu_custom_call" | custom-call | tf_op jit(solution)/shard_map/pallas_call | solution.py:279
  46.4 0.0 copy-start
  46.4 1.7 %copy.12 = f32[8,16,512]{2,1,0:T(8,128)} copy(f32[8,16,512]{2,1,0:T(8,128)} %get-tuple-element.4) | data formatting | bytes 524288
  48.1 0.0 copy-done
  48.1 0.7 %copy.13 = f32[8,16,512]{2,1,0:T(8,128)} copy(f32[8,16,512]{2,1,0:T(8,128)S(1)} %copy-done) | data formatting | bytes 524288
Async XLA Ops:
  46.4 1.7 %copy-start = (f32[8,16,512]{2,1,0:T(8,128)S(1)}, f32[8,16,512]{2,1,0:T(8,128)}, u32[]{:S(2)}) copy-start(f32[8,16,512]{2,1,0:T(8,128)} %get-tuple-element.5) | copy-start | bytes 786436
